TPU v7x, 128 devices: a whole 4x4x4 slice. The times are simulated.
128 devices in a mesh: task: 4 (over y_hi, core), row: 32 (over x, y_lo, z).
Axes of the slice: x: 4, y: 4 (y_hi: 2, y_lo: 2; y = y_hi * 2 + y_lo), z: 4, core: 2. Of those that a mesh axis runs over, the one named last changes fastest.
Arguments:
- deltas: bfloat16 [8, 25600, 5120], P('task', 'row'), may hold values from -20 to 20, as said below
- sketch: bfloat16 [25600, 128], P('row'), may hold values from -0.0390625 to 0.0390625
Outputs:
- merged: bfloat16 [25600, 5120], P('row', 'task')
Inputs may be any that keep to these rules, and one draw needn't show every extreme that they name: Real-valued deltas; the tasks share part of their structure.
All inputs are finite; a program needn't handle non-finite values.
Results may differ from a plain program's by a relative error of at most 0.04.
Values may be sent and summed in bfloat16 or wider, within the bound.
No kernel may reach another device: no remote copies, remote signals or barrier semaphores. Data moves between devices by JAX's collectives and lax.ppermute only.
A program may use at most 128 MiB of HBM per device.

v0:
```python
import jax
import jax.numpy as jnp
from jax import lax
from jax.sharding import PartitionSpec as P

NS_STEPS = 5


def body(deltas, sketch):
    local_tasks = deltas.shape[0]
    local_rows = deltas.shape[1]
    model_width = deltas.shape[2]
    rank_width = sketch.shape[1]
    group_count = lax.axis_size("task")
    row_devices = lax.axis_size("row")
    basis_rows_dev = model_width // row_devices
    group_width = local_tasks * rank_width
    basis_width = group_width * group_count
    gram_rows_dev = basis_width // row_devices
    terms = jnp.einsum("tmk,mr->ktr", deltas, sketch, preferred_element_type=jnp.float32)
    basis_local = lax.psum_scatter(
        terms.reshape(basis_rows_dev * lax.axis_size("row"), group_width).astype(jnp.bfloat16),
        "row",
        scatter_dimension=0,
        tiled=True,
    )
    basis_block = lax.all_gather(basis_local, "task", axis=1, tiled=True)
    gram_local = lax.psum_scatter(
        jnp.einsum(
            "kc,kp->cp", basis_block, basis_local, preferred_element_type=jnp.float32
        ).astype(jnp.bfloat16),
        "row",
        scatter_dimension=0,
        tiled=True,
    ).astype(jnp.float32)
    gram_own = lax.all_gather(gram_local.astype(jnp.bfloat16), "task", axis=1, tiled=True).astype(
        gram_local.dtype
    )
    frob = jnp.sqrt(lax.psum(jnp.sum(gram_own * gram_own), "row"))
    rows_y = (gram_own / frob).astype(jnp.bfloat16)
    first_row = lax.axis_index("row") * gram_rows_dev
    row_ids = lax.broadcasted_iota(jnp.int32, (gram_rows_dev, basis_width), 0) + first_row
    col_ids = lax.broadcasted_iota(jnp.int32, (gram_rows_dev, basis_width), 1)
    identity_rows = jnp.where(row_ids == col_ids, 1.0, 0.0).astype(jnp.float32)
    turn_rows = ((3.0 * identity_rows - rows_y.astype(jnp.float32)) * 0.5).astype(jnp.bfloat16)
    whole_turn = lax.all_gather(turn_rows, "row", axis=0, tiled=True)
    rows_y = jnp.dot(rows_y, whole_turn, preferred_element_type=jnp.float32).astype(jnp.bfloat16)
    rows_z = turn_rows
    for iteration in range(1, NS_STEPS):
        whole_y, whole_z = (
            lax.all_gather(rows_y, "row", axis=0, tiled=True),
            lax.all_gather(rows_z, "row", axis=0, tiled=True),
        )
        turn = (
            (3.0 * identity_rows - jnp.dot(rows_z, whole_y, preferred_element_type=jnp.float32))
            * 0.5
        ).astype(jnp.bfloat16)
        if iteration + 1 < NS_STEPS:
            rows_y = jnp.dot(turn, whole_y, preferred_element_type=jnp.float32).astype(jnp.bfloat16)
        rows_z = jnp.dot(turn, whole_z, preferred_element_type=jnp.float32).astype(jnp.bfloat16)
    inverse_root = lax.all_gather(rows_z, "row", axis=0, tiled=True)
    basis_whole = lax.all_gather(basis_block, "row", axis=0, tiled=True)
    task_total = local_tasks * group_count
    coeff_part = jnp.zeros((local_rows, basis_width), jnp.float32)
    for task_slot in range(local_tasks):
        coeff_part = coeff_part + jnp.dot(
            deltas[task_slot], basis_whole, preferred_element_type=jnp.float32
        )
    coeff = (
        lax.psum(coeff_part.astype(jnp.bfloat16), "task").astype(jnp.float32) / task_total
    ).astype(jnp.bfloat16)
    second = jnp.dot(coeff, inverse_root, preferred_element_type=jnp.float32).astype(jnp.bfloat16)
    third = (jnp.dot(second, inverse_root, preferred_element_type=jnp.float32) / frob).astype(
        jnp.bfloat16
    )
    column_width = model_width // group_count
    column_basis = lax.dynamic_slice_in_dim(
        basis_whole, lax.axis_index("task") * column_width, column_width, 0
    )
    return jnp.einsum("mc,kc->mk", third, column_basis, preferred_element_type=jnp.float32).astype(
        jnp.bfloat16
    )


def solution(mesh):
    return jax.shard_map(
        body,
        mesh=mesh,
        in_specs=(P("task", "row", None), P("row", None)),
        out_specs=P("row", "task"),
        check_vma=False,
    )
```

profile of v0, /device:TPU:1, one launch (start us, length us, event | category | flops | bytes accessed | tf_op | source)
XLA Modules:
  0.0 2060.8 jit_solution(4561079936277309)
XLA Ops:
  6.5 0.9 copy-done
  7.5 8.7 convolution_convert_fusion
  16.1 2.6 copy.4
  18.8 0.0 reduce-scatter.7.cloned.1.call-update
  18.8 0.0 reduce-scatter.5.cloned.1.call-start
  18.9 144.4 %reduce-scatter.7.cloned.1.call-done = bf16[160,256]{1,0:T(8,128)(2,1)} async-done(((bf16[5120,256]{1,0:T(8,128)(2,1)}), bf16[160,256]{1,0:T(8,128)(2,1)}) %reduce-scatter.7.cloned.1.call-update) | async-done | bytes 81936
  163.3 1.0 copy.5
  164.2 32.8 %all_gather.37 = bf16[160,1024]{0,1:T(8,128)(2,1)S(1)} all-gather(bf16[160,256]{0,1:T(8,128)(2,1)S(1)} %copy.5), channel_id=1, replica_groups=mesh['task'=4,'row'=32] {'task'}, dimensions={1}, use_global_device_ids=true | all-gather | bytes 409600 | tf_op jit(solution)/shard_map/all_gather | solution.py:27
  197.0 2.0 convolution_convert_fusion.2
  199.0 0.0 reduce-scatter.5.cloned.1.call-update
  199.0 0.0 all-gather.13.cloned.1.call-start
  199.0 130.0 %reduce-scatter.5.cloned.1.call-done = bf16[32,256]{1,0:T(8,128)(2,1)} async-done(((bf16[1024,256]{1,0:T(8,128)(2,1)}), bf16[32,256]{1,0:T(8,128)(2,1)}) %reduce-scatter.5.cloned.1.call-update) | async-done | bytes 16400 | tf_op jit(solution)/shard_map/reduce_scatter | solution.py:28
  329.1 32.8 %all_gather.39 = bf16[32,1024]{1,0:T(8,128)(2,1)S(1)} all-gather(bf16[32,256]{1,0:T(8,128)(2,1)} %reduce-scatter.5.cloned.1.call-done), channel_id=1, replica_groups=mesh['task'=4,'row'=32] {'task'}, dimensions={1}, use_global_device_ids=true | all-gather | bytes 81920 | tf_op jit(solution)/shard_map/all_gather | solution.py:36
  361.8 0.6 fusion.24
  362.5 64.5 %psum.15 = f32[]{:T(128)} all-reduce(f32[]{:T(128)} %fusion.24), channel_id=1, replica_groups=mesh['task'=4,'row'=32] {'row'}, use_global_device_ids=true, to_apply=%region_4.5 | all-reduce | flops 1 | bytes 8 | tf_op jit(solution)/shard_map/psum | solution.py:39
  427.7 0.7 multiply_convert_fusion.6
  428.4 0.0 all-gather.13.cloned.1.call-update
  428.4 0.0 all-gather.15.cloned.1.call-start
  428.5 142.5 %all-gather.13.cloned.1.call-done = bf16[1024,1024]{1,0:T(8,128)(2,1)} async-done(((bf16[32,1024]{1,0:T(8,128)(2,1)}), bf16[1024,1024]{1,0:T(8,128)(2,1)}) %all-gather.13.cloned.1.call-update) | async-done | bytes 2097168 | tf_op jit(solution)/shard_map/all_gather | solution.py:46
  571.0 2.7 convolution_convert_fusion.10
  573.7 0.0 all-gather.15.cloned.1.call-update
  573.7 0.0 all-gather.17.cloned.1.call-start
  573.8 153.2 %all-gather.15.cloned.1.call-done = bf16[1024,1024]{1,0:T(8,128)(2,1)} async-done(((bf16[32,1024]{1,0:T(8,128)(2,1)}), bf16[1024,1024]{1,0:T(8,128)(2,1)}) %all-gather.15.cloned.1.call-update) | async-done | bytes 2097168 | tf_op jit(solution)/shard_map/all_gather | solution.py:51
  727.0 2.1 fusion.19
  729.0 2.7 convolution_convert_fusion.8
  731.7 0.0 all-gather.17.cloned.1.call-update
  731.8 0.0 all-gather.19.cloned.1.call-start
  731.8 1.1 convolution_convert_fusion.9
  732.9 0.0 all-gather.19.cloned.1.call-update
  732.9 0.0 all-gather.21.cloned.1.call-start
  733.0 152.0 %all-gather.17.cloned.1.call-done = bf16[1024,1024]{1,0:T(8,128)(2,1)} async-done(((bf16[32,1024]{1,0:T(8,128)(2,1)}), bf16[1024,1024]{1,0:T(8,128)(2,1)}) %all-gather.17.cloned.1.call-update) | async-done | bytes 2097168 | tf_op jit(solution)/shard_map/all_gather | solution.py:51
  885.0 2.2 fusion.20
  887.3 1.1 convolution_convert_fusion.6
  888.4 0.0 all-gather.21.cloned.1.call-update
  888.4 0.0 all-gather.23.cloned.1.call-start
  888.5 151.3 %all-gather.19.cloned.1.call-done = bf16[1024,1024]{1,0:T(8,128)(2,1)} async-done(((bf16[32,1024]{1,0:T(8,128)(2,1)}), bf16[1024,1024]{1,0:T(8,128)(2,1)}) %all-gather.19.cloned.1.call-update) | async-done | bytes 2097168 | tf_op jit(solution)/shard_map/all_gather | solution.py:52
  1039.7 2.7 convolution_convert_fusion.7
  1042.4 0.0 all-gather.23.cloned.1.call-update
  1042.4 0.0 all-gather.11.cloned.1.call-start
  1042.5 0.9 copy.3
  1043.4 0.0 all-gather.11.cloned.1.call-update
  1043.4 0.0 all-gather.25.cloned.1.call-start
  1043.5 151.1 %all-gather.21.cloned.1.call-done = bf16[1024,1024]{1,0:T(8,128)(2,1)} async-done(((bf16[32,1024]{1,0:T(8,128)(2,1)}), bf16[1024,1024]{1,0:T(8,128)(2,1)}) %all-gather.21.cloned.1.call-update) | async-done | bytes 2097168 | tf_op jit(solution)/shard_map/all_gather | solution.py:51
  1194.6 2.2 fusion.21
  1196.8 1.1 convolution_convert_fusion.4
  1197.9 0.0 all-gather.25.cloned.1.call-update
  1198.0 0.0 all-gather.27.cloned.1.call-start
  1198.0 151.4 %all-gather.23.cloned.1.call-done = bf16[1024,1024]{1,0:T(8,128)(2,1)} async-done(((bf16[32,1024]{1,0:T(8,128)(2,1)}), bf16[1024,1024]{1,0:T(8,128)(2,1)}) %all-gather.23.cloned.1.call-update) | async-done | bytes 2097168 | tf_op jit(solution)/shard_map/all_gather | solution.py:52
  1349.4 2.7 convolution_convert_fusion.5
  1352.1 0.0 all-gather.27.cloned.1.call-update
  1352.2 0.2 all-reduce.2.cloned.1.call-start
  1352.4 172.2 %all-gather.11.cloned.1.call-done = bf16[5120,1024]{1,0:T(8,128)(2,1)} async-done(((bf16[160,1024]{1,0:T(8,128)(2,1)}), bf16[5120,1024]{1,0:T(8,128)(2,1)}) %all-gather.11.cloned.1.call-update) | async-done | bytes 10485776 | tf_op jit(solution)/shard_map/all_gather | solution.py:62
  1524.6 15.0 fusion
  1539.6 17.2 fusion.12
  1556.8 0.0 all-reduce.2.cloned.1.call-update
  1556.8 0.3 all-gather.29.cloned.1.call-start
  1557.1 118.7 %all-gather.25.cloned.1.call-done = bf16[1024,1024]{1,0:T(8,128)(2,1)} async-done(((bf16[32,1024]{1,0:T(8,128)(2,1)}), bf16[1024,1024]{1,0:T(8,128)(2,1)}) %all-gather.25.cloned.1.call-update) | async-done | bytes 2097168 | tf_op jit(solution)/shard_map/all_gather | solution.py:51
  1675.8 154.9 %all-gather.27.cloned.1.call-done = bf16[1024,1024]{1,0:T(8,128)(2,1)} async-done(((bf16[32,1024]{1,0:T(8,128)(2,1)}), bf16[1024,1024]{1,0:T(8,128)(2,1)}) %all-gather.27.cloned.1.call-update) | async-done | bytes 2097168 | tf_op jit(solution)/shard_map/all_gather | solution.py:52
  1830.7 3.7 convolution_convert_fusion.3
  1834.4 0.0 all-gather.29.cloned.1.call-update
  1834.4 74.6 %all-reduce.2.cloned.1.call-done = bf16[800,1024]{0,1:T(8,128)(2,1)} async-done(((bf16[800,1024]{0,1:T(8,128)(2,1)}), bf16[800,1024]{0,1:T(8,128)(2,1)}) %all-reduce.2.cloned.1.call-update) | async-done | bytes 1638416 | tf_op jit(solution)/shard_map/psum | solution.py:70
  1909.0 133.4 %all-gather.29.cloned.1.call-done = bf16[1024,1024]{1,0:T(8,128)(2,1)} async-done(((bf16[32,1024]{1,0:T(8,128)(2,1)}), bf16[1024,1024]{1,0:T(8,128)(2,1)}) %all-gather.29.cloned.1.call-update) | async-done | bytes 2097168 | tf_op jit(solution)/shard_map/all_gather | solution.py:61
  2042.5 6.4 divide_convert_fusion
  2048.9 5.4 convolution_convert_fusion.1
  (13 shorter events, 0.0 us)
Async XLA Ops:
  6.5 0.9 copy-start
  6.5 156.7 %reduce-scatter.7.cloned.1.call-start = ((), (), s32[]{:S(2)}) async-start(), calls=%async_computation.14 | async-start | bytes 2703360
  18.8 310.3 %reduce-scatter.5.cloned.1.call-start = ((), (), s32[]{:S(2)}) async-start(), calls=%async_computation.4 | async-start | bytes 540672 | tf_op jit(solution)/shard_map/reduce_scatter | solution.py:28
  199.0 372.0 %all-gather.13.cloned.1.call-start = ((), (), s32[]{:S(2)}) async-start(), calls=%async_computation.5 | async-start | bytes 2162688 | tf_op jit(solution)/shard_map/all_gather | solution.py:46
  428.4 298.6 %copy-start.5 = (bf16[32,1024]{1,0:T(8,128)(2,1)S(1)}, bf16[32,1024]{1,0:T(8,128)(2,1)}, u32[]{:S(2)}) copy-start(bf16[32,1024]{1,0:T(8,128)(2,1)} %multiply_convert_fusion.6) | copy-start | bytes 196612
  428.4 298.6 %all-gather.15.cloned.1.call-start = ((), (), s32[]{:S(2)}) async-start(), calls=%async_computation.6 | async-start | bytes 2162688 | tf_op jit(solution)/shard_map/all_gather | solution.py:51
  573.7 158.1 %copy-start.2 = (bf16[1024,1024]{1,0:T(8,128)(2,1)S(1)}, bf16[1024,1024]{1,0:T(8,128)(2,1)}, u32[]{:S(2)}) copy-start(bf16[1024,1024]{1,0:T(8,128)(2,1)} %all-gather.13.cloned.1.call-done) | copy-start | bytes 6291460
  573.7 311.3 %all-gather.17.cloned.1.call-start = ((), (), s32[]{:S(2)}) async-start(), calls=%async_computation.7 | async-start | bytes 2162688 | tf_op jit(solution)/shard_map/all_gather | solution.py:51
  731.8 308.0 %all-gather.19.cloned.1.call-start = ((), (), s32[]{:S(2)}) async-start(), calls=%async_computation.8 | async-start | bytes 2162688 | tf_op jit(solution)/shard_map/all_gather | solution.py:52
  732.9 461.6 %all-gather.21.cloned.1.call-start = ((), (), s32[]{:S(2)}) async-start(), calls=%async_computation.9 | async-start | bytes 2162688 | tf_op jit(solution)/shard_map/all_gather | solution.py:51
  885.0 2.3 copy-start.3
  888.4 461.0 %all-gather.23.cloned.1.call-start = ((), (), s32[]{:S(2)}) async-start(), calls=%async_computation.10 | async-start | bytes 2162688 | tf_op jit(solution)/shard_map/all_gather | solution.py:52
  1042.4 482.2 %all-gather.11.cloned.1.call-start = ((), (), s32[]{:S(2)}) async-start(), calls=%async_computation.2 | async-start | bytes 10813440 | tf_op jit(solution)/shard_map/all_gather | solution.py:62
  1043.4 632.4 %all-gather.25.cloned.1.call-start = ((), (), s32[]{:S(2)}) async-start(), calls=%async_computation.11 | async-start | bytes 2162688 | tf_op jit(solution)/shard_map/all_gather | solution.py:51
  1194.6 2.3 copy-start.1
  1198.0 632.7 %all-gather.27.cloned.1.call-start = ((), (), s32[]{:S(2)}) async-start(), calls=%async_computation.12 | async-start | bytes 2162688 | tf_op jit(solution)/shard_map/all_gather | solution.py:52
  1352.2 556.9 %all-reduce.2.cloned.1.call-start = ((), (), s32[]{:S(2)}) async-start(), calls=%async_computation.3 | async-start | bytes 3670016 | tf_op jit(solution)/shard_map/psum | solution.py:70
  1539.6 291.1 %copy-start.4 = (bf16[32,1024]{1,0:T(8,128)(2,1)S(1)}, bf16[32,1024]{1,0:T(8,128)(2,1)}, u32[]{:S(2)}) copy-start(bf16[32,1024]{1,0:T(8,128)(2,1)} %convolution_convert_fusion.5) | copy-start | bytes 196612
  1556.8 485.7 %all-gather.29.cloned.1.call-start = ((), (), s32[]{:S(2)}) async-start(), calls=%async_computation.13 | async-start | bytes 2162688 | tf_op jit(solution)/shard_map/all_gather | solution.py:61
Sparse Core Ops, SparseCore 0:
  18.9 144.2 reduce-scatter.6
  199.1 129.9 reduce-scatter.4
  428.5 142.4 all-gather.12
  573.8 153.0 all-gather.14
  731.9 153.0 all-gather.16
  886.6 153.0 all-gather.18
  1041.5 153.0 all-gather.20
  1196.3 153.0 all-gather.22
  1351.2 173.3 all-gather.10
  1526.2 149.6 all-gather.24
  1677.6 153.0 all-gather.26
  1833.2 75.7 all-reduce.1
  1910.8 131.6 all-gather.28
where the time goes:
time: 2080 us; the launch traced here: 2060 us
  waiting for transfers between devices  1830 us (88%)
  blocking collectives  130 us (6%)
  matrix products  78.9 us (4%)
    all_gather x4, waiting for transfers between devices, body(): lax.all_gather(rows_y, 'row', axis=0, tiled=True)  575 us
    all_gather x3, waiting for transfers between devices, body(): lax.all_gather(rows_z, 'row', axis=0, tiled=True)  458 us
    all_gather x1, waiting for transfers between devices, body(): basis_whole = lax.all_gather(basis_block, 'row', axis=0, tiled=True)  172 us
    unnamed x14, waiting for transfers between devices  145 us
    all_gather x1, waiting for transfers between devices, body(): whole_turn = lax.all_gather(turn_rows, 'row', axis=0, tiled=True)  143 us
    all_gather x1, waiting for transfers between devices, body(): inverse_root = lax.all_gather(rows_z, 'row', axis=0, tiled=True)  133 us
    reduce_scatter x1, waiting for transfers between devices, body(): lax.psum_scatter(jnp.einsum('kc,kp->cp', basis_block, basis_local, prefer...  130 us
    psum x1, waiting for transfers between devices, body(): lax.psum(coeff_part.astype(jnp.bfloat16), 'task').astype(jnp.float32)  74.6 us
  transfers between devices with their start and end apart: 13, of which 13 were waited for; matrix products, arithmetic and copies ran while one was open for 2% of the time, Pallas kernels for 0%

commit v1 on v0

v1 whole, which is shorter than its diff:
```python
import jax
import jax.numpy as jnp
from jax import lax
from jax.experimental import pallas as pl
from jax.experimental.pallas import tpu as pltpu
from jax.sharding import Mesh
from jax.sharding import PartitionSpec as P

NS_STEPS = 5
BF = jnp.bfloat16
F32 = jnp.float32
VMEM_LIMIT = 60 * 1024 * 1024
RING_Y = ("yh", "yl")
SAME_CORE = ("yh", "x", "yl", "z")


def params():
    return pltpu.CompilerParams(vmem_limit_bytes=VMEM_LIMIT)


def whole():
    return pl.BlockSpec(memory_space=pltpu.VMEM)


def shift(value, axis, step):
    size = lax.axis_size(axis)
    return lax.ppermute(value, axis, [(i, (i + step) % size) for i in range(size)])


def sketch_kernel(core_ref, deltas_ref, sketch_ref, out_ref, pool_ref):
    quarter = pl.program_id(0)
    rank = sketch_ref.shape[1]
    for task in range(deltas_ref.shape[0]):
        part = lax.dot_general(
            sketch_ref[...], deltas_ref[task], (((0,), (0,)), ((), ())), preferred_element_type=F32
        )
        rows = part.T.astype(BF)
        rows = rows.reshape(out_ref.shape[1], out_ref.shape[3], rank)
        out_ref[0, :, 0, :, task * rank : (task + 1) * rank] = rows

    @pl.when(quarter % 2 != core_ref[0])
    def _():
        pool_ref[0] = (deltas_ref[0].astype(F32) + deltas_ref[1].astype(F32)).astype(BF)


def sketch_call(core, deltas, sketch):
    tasks, rows, width = deltas.shape
    rank = sketch.shape[1]
    quarter = width // 4
    return pl.pallas_call(
        sketch_kernel,
        grid_spec=pltpu.PrefetchScalarGridSpec(
            num_scalar_prefetch=1,
            grid=(4,),
            in_specs=[
                pl.BlockSpec((tasks, rows, quarter), lambda i, c: (0, 0, i)),
                pl.BlockSpec((rows, rank), lambda i, c: (0, 0)),
            ],
            out_specs=[
                pl.BlockSpec((1, 4, 1, quarter // 4, tasks * rank), lambda i, c: (i // 2, 0, i % 2, 0, 0)),
                pl.BlockSpec((1, rows, quarter), lambda i, c: (i // 2, 0, 0)),
            ],
        ),
        out_shape=[
            jax.ShapeDtypeStruct((2, 4, 2, quarter // 4, tasks * rank), BF),
            jax.ShapeDtypeStruct((2, rows, quarter), BF),
        ],
        compiler_params=params(),
        name="sketch",
    )(core, deltas, sketch)


def gram_kernel(at_ref, a0, a1, a2, a3, a4, b0, b1, b2, b3, b4, basis_ref, gram_ref):
    x, z = at_ref[0], at_ref[1]
    half = a0.shape[3]

    def place(src, own_shift, src_first, count, columns, along_z):
        for j in range(count):
            inner = (0, -1, 1, 2)[src_first + j]
            outer_at = lax.rem((z if along_z else x) + own_shift + 4, 4)
            inner_at = lax.rem((x if along_z else z) + inner + 4, 4)
            xi, zi = (inner_at, outer_at) if along_z else (outer_at, inner_at)
            for h in range(2):
                basis_ref[h, xi, zi, :, columns] = src[j, h]

    for refs, columns, along_z in (
        ((a0, a1, a2, a3, a4), slice(0, half), True),
        ((b0, b1, b2, b3, b4), slice(half, 2 * half), False),
    ):
        place(refs[0], 0, 0, 4, columns, along_z)
        place(refs[1], -1, 0, 4, columns, along_z)
        place(refs[2], 1, 0, 4, columns, along_z)
        place(refs[3], 2, 0, 2, columns, along_z)
        place(refs[4], 2, 2, 2, columns, along_z)

    depth = 2 * 16 * a0.shape[2]
    width = 2 * half
    block = 256
    right = basis_ref[...].reshape(depth, width)
    for i in range(width // block):
        left = basis_ref[:, :, :, :, i * block : (i + 1) * block].reshape(depth, block)
        gram_ref[i * block : (i + 1) * block, :] = lax.dot_general(
            left, right, (((0,), (0,)), ((), ())), preferred_element_type=F32
        ).astype(BF)


def gram_call(at, parts):
    _, _, rows, half = parts[0].shape
    return pl.pallas_call(
        gram_kernel,
        in_specs=[pl.BlockSpec(memory_space=pltpu.SMEM)] + [whole()] * 10,
        out_specs=[whole(), whole()],
        out_shape=[
            jax.ShapeDtypeStruct((2, 4, 4, rows, 2 * half), BF),
            jax.ShapeDtypeStruct((2 * half, 2 * half), BF),
        ],
        compiler_params=params(),
        name="gram",
    )(at, *parts)


def coeff_kernel(core_ref, deltas_ref, pool_ref, basis_ref, out_ref, acc_ref):
    step = pl.program_id(0)
    pooled = (
        deltas_ref[0].astype(F32) + deltas_ref[1].astype(F32) + pool_ref[0].astype(F32)
    ).astype(BF)
    part = jnp.dot(pooled, basis_ref[0], preferred_element_type=F32)

    @pl.when(step == 0)
    def _():
        acc_ref[...] = part

    @pl.when(step == 1)
    def _():
        out_ref[...] = (acc_ref[...] + part).astype(BF)


def coeff_call(core, deltas, pool, basis):
    tasks, rows, width = deltas.shape
    quarter = width // 4
    columns = basis.shape[2]
    return pl.pallas_call(
        coeff_kernel,
        grid_spec=pltpu.PrefetchScalarGridSpec(
            num_scalar_prefetch=1,
            grid=(2,),
            in_specs=[
                pl.BlockSpec((tasks, rows, quarter), lambda i, c: (0, 0, 2 * i + c[0])),
                pl.BlockSpec((1, rows, quarter), lambda i, c: (i, 0, 0)),
                pl.BlockSpec((1, quarter, columns), lambda i, c: (i, 0, 0)),
            ],
            out_specs=pl.BlockSpec((rows, columns), lambda i, c: (0, 0)),
            scratch_shapes=[pltpu.VMEM((rows, columns), F32)],
        ),
        out_shape=jax.ShapeDtypeStruct((rows, columns), BF),
        compiler_params=params(),
        name="coeff",
    )(core, deltas, pool, basis)


def schulz_kernel(own_ref, other_ref, z_ref, frob_ref, y_ref, t_ref, y2_ref, z2_ref):
    size = own_ref.shape[0]
    block = 256
    blocks = size // block

    total = jnp.zeros((8, size), F32)
    for i in range(blocks):
        rows = slice(i * block, (i + 1) * block)
        gram = own_ref[rows, :].astype(F32) + other_ref[rows, :].astype(F32)
        total = total + jnp.sum((gram * gram).reshape(block // 8, 8, size), axis=0)
    frob = jnp.sqrt(jnp.sum(total, keepdims=True))
    frob_ref[...] = jnp.broadcast_to(frob, frob_ref.shape)

    def turn_of(value, first_row, first_col):
        row = lax.broadcasted_iota(jnp.int32, value.shape, 0) + first_row
        col = lax.broadcasted_iota(jnp.int32, value.shape, 1) + first_col
        return ((jnp.where(row == col, 3.0, 0.0) - value) * 0.5).astype(BF)

    for i in range(blocks):
        rows = slice(i * block, (i + 1) * block)
        gram = own_ref[rows, :].astype(F32) + other_ref[rows, :].astype(F32)
        y = (gram / frob).astype(BF)
        y_ref[rows, :] = y
        t_ref[rows, :] = turn_of(y.astype(F32), i * block, 0)

    def product(left, right, out, turn):
        @pl.loop(0, blocks)
        def _(j):
            columns = pl.ds(pl.multiple_of(j * block, block), block)
            value = jnp.dot(left[...], right[:, columns], preferred_element_type=F32)
            out[:, columns] = turn_of(value, 0, j * block) if turn else value.astype(BF)

    product(y_ref, t_ref, y2_ref, False)
    z2_ref[...] = t_ref[...]
    y_now, z_now, y_next, z_next = y2_ref, z2_ref, y_ref, z_ref
    for iteration in range(1, NS_STEPS):
        product(z_now, y_now, t_ref, True)
        if iteration + 1 < NS_STEPS:
            product(t_ref, y_now, y_next, False)
        product(t_ref, z_now, z_next, False)
        y_now, y_next = y_next, y_now
        z_now, z_next = z_next, z_now
    if z_now is not z_ref:
        z_ref[...] = z_now[...]


def schulz_call(own, other):
    size = own.shape[0]
    square = (size, size)
    return pl.pallas_call(
        schulz_kernel,
        in_specs=[whole(), whole()],
        out_specs=[whole(), whole()],
        out_shape=[jax.ShapeDtypeStruct(square, BF), jax.ShapeDtypeStruct((8, 128), F32)],
        scratch_shapes=[pltpu.VMEM(square, BF)] * 4,
        cost_estimate=pl.CostEstimate(flops=24 * size**3, bytes_accessed=6 * size**2, transcendentals=0),
        compiler_params=params(),
        name="schulz",
    )(own, other)


def merge_kernel(coeff_ref, z_ref, frob_ref, basis_ref, out_ref):
    second = jnp.dot(coeff_ref[...], z_ref[...], preferred_element_type=F32).astype(BF)
    third = jnp.dot(second, z_ref[...], preferred_element_type=F32)
    third = (third / frob_ref[0:1, 0:1]).astype(BF)
    out_ref[...] = lax.dot_general(
        third, basis_ref[0], (((1,), (1,)), ((), ())), preferred_element_type=F32
    ).astype(BF)


def merge_call(yh, coeff, z, frob, basis):
    rows, width = coeff.shape
    columns = basis.shape[1]
    block = rows // 2
    return pl.pallas_call(
        lambda at, *refs: merge_kernel(*refs),
        grid_spec=pltpu.PrefetchScalarGridSpec(
            num_scalar_prefetch=1,
            grid=(2,),
            in_specs=[
                pl.BlockSpec((block, width), lambda i, h: (i, 0)),
                pl.BlockSpec((width, width), lambda i, h: (0, 0)),
                pl.BlockSpec((8, 128), lambda i, h: (0, 0)),
                pl.BlockSpec((1, columns, width), lambda i, h: (h[0], 0, 0)),
            ],
            out_specs=pl.BlockSpec((block, columns), lambda i, h: (i, 0)),
        ),
        out_shape=jax.ShapeDtypeStruct((rows, columns), BF),
        compiler_params=params(),
        name="merge",
    )(yh, coeff, z, frob, basis)


def ring_gather(items):
    first = [(shift(a, axis, 1), shift(a, axis, -1)) for a, axis in items]
    out = []
    for (a, axis), (before, after) in zip(items, first):
        cut = a.shape[0] // 2
        low = shift(before[:cut], axis, 1)
        high = shift(after[cut:], axis, -1)
        out.append((a, before, after, low, high))
    return out


def body(deltas, sketch):
    tasks, rows, width = deltas.shape
    core, yh, yl = lax.axis_index("core"), lax.axis_index("yh"), lax.axis_index("yl")
    x, z = lax.axis_index("x"), lax.axis_index("z")
    core1 = core.astype(jnp.int32).reshape(1)

    terms, pool_out = sketch_call(core1, deltas, sketch)
    pool_in = shift(pool_out, "core", 1)

    chips = 64
    piece = width // chips
    group_width = terms.shape[-1]
    arrived = lax.all_to_all(
        terms.reshape(chips, piece, group_width), SAME_CORE, 0, 0, tiled=True
    )
    summed = jnp.sum(arrived.reshape(2, chips // 2, piece, group_width).astype(F32), axis=1).astype(BF)
    own = jnp.concatenate([summed[0], summed[1]], axis=1)

    below, above, across = shift(own, RING_Y, 1), shift(own, RING_Y, -1), shift(own, RING_Y, 2)
    near = jnp.where(yl == 0, above, below)
    far = jnp.where(yl == 0, below, above)
    low_first = yh == 0
    same = jnp.stack([jnp.where(low_first, own, across), jnp.where(low_first, across, own)])
    other = jnp.stack([jnp.where(low_first, near, far), jnp.where(low_first, far, near)])
    keep = jnp.where(yl == core, same, other)
    give = jnp.where(yl == core, other, same)
    got = shift(give, "core", 1)
    part_a = jnp.where(core == 0, keep, got)
    part_b = jnp.where(core == 0, got, keep)

    mid = ring_gather([(part_a, "x"), (part_b, "z")])
    stacked = [
        jnp.stack([m[0], m[1], m[2], jnp.concatenate([m[3], m[4]], axis=0)]) for m in mid
    ]
    last = ring_gather([(stacked[0], "z"), (stacked[1], "x")])
    at = jnp.stack([x, z]).astype(jnp.int32)
    basis, gram_own = gram_call(at, [*last[0], *last[1]])
    basis = basis.reshape(2, width // 4, basis.shape[-1])

    gram_other = shift(gram_own, "core", 1)
    coeff_part = coeff_call(core1, deltas, pool_in, basis)

    half = rows // 2
    mine = lax.dynamic_slice_in_dim(coeff_part, core * half, half, 0)
    give = lax.dynamic_slice_in_dim(coeff_part, (1 - core) * half, half, 0)
    chip_sum = (mine.astype(F32) + shift(give, "core", 1).astype(F32)).astype(BF)
    over = shift(chip_sum, "yh", 1)
    total_tasks = tasks * lax.axis_size("yh") * lax.axis_size("core")
    coeff_half = ((chip_sum.astype(F32) + over.astype(F32)) / total_tasks).astype(BF)
    coeff_twin = shift(coeff_half, "core", 1)
    coeff = jnp.concatenate(
        [jnp.where(core == 0, coeff_half, coeff_twin), jnp.where(core == 0, coeff_twin, coeff_half)]
    )

    inverse_root, frob = schulz_call(gram_own, gram_other)
    return merge_call(yh.astype(jnp.int32).reshape(1), coeff, inverse_root, frob, basis)


def solution(mesh):
    fine = Mesh(mesh.devices.reshape(2, 2, 4, 2, 4), ("yh", "core", "x", "yl", "z"))
    task, row = ("yh", "core"), ("x", "yl", "z")
    return jax.shard_map(
        body,
        mesh=fine,
        in_specs=(P(task, row, None), P(row, None)),
        out_specs=P(row, task),
        check_vma=False,
    )
```

time: 2080 us -> 216 us (0.10)
  waiting for transfers between devices: 1830 us -> 76.4 us
  blocking collectives: 130 us -> 0 us
  Pallas kernels: 0 us -> 82.4 us
  matrix products: 78.9 us -> 0 us
  starting transfers between devices: 0.91 us -> 48.3 us
    all_gather x10 -> x0, waiting for transfers between devices: 1480 us -> none  [the longest x4 575 us: body(): lax.all_gather(rows_y, 'row', axis=0, tiled=True)]
    unnamed x14 -> x0, waiting for transfers between devices: 145 us -> none
    reduce_scatter x1 -> x0, waiting for transfers between devices: 130 us -> none  [body(): lax.psum_scatter(jnp.einsum('kc,kp->cp', basis_block, basis_local, prefer...]
    pallas_call x0 -> x5, Pallas kernels: none -> 82.4 us  [the longest x1 42 us: schulz_call(): pl.pallas_call(schulz_kernel, in_specs=[whole(), whole()], out_specs=[who...]
    dot_general x17 -> x0, matrix products: 78.9 us -> none  [the longest x2 32.2 us: body(): jnp.dot(deltas[task_slot], basis_whole, preferred_element_type=jnp.float32)]
    psum x1 -> x0, waiting for transfers between devices: 74.6 us -> none  [body(): lax.psum(coeff_part.astype(jnp.bfloat16), 'task').astype(jnp.float32)]
    all_gather x2 -> x0, blocking collectives: 65.5 us -> none  [the longest x1 32.8 us: body(): lax.all_gather(gram_local.astype(jnp.bfloat16), 'task', axis=1, tiled=True)]
    psum x1 -> x0, blocking collectives: 64.5 us -> none  [body(): frob = jnp.sqrt(lax.psum(jnp.sum(gram_own * gram_own), 'row'))]
  transfers between devices with their start and end apart: 13 -> 26, of which waited for: 13 -> 13; matrix products, arithmetic and copies ran while one was open for 2% -> 2% of each run, Pallas kernels for 0% -> 24%
where the time goes in v1:
time: 216 us
  Pallas kernels  82.4 us (38%)
  waiting for transfers between devices  76.4 us (35%)
  starting transfers between devices  48.3 us (22%)
  local copies, waits for them, and re-layouts  5.37 us (2%)
  other arithmetic  3.42 us (2%)
    ppermute x25, waiting for transfers between devices, shift(): lax.ppermute(value, axis, [(i, (i + step) % size) for i in range(size)])  45.8 us
    pallas_call x1, Pallas kernels, schulz_call(): pl.pallas_call(schulz_kernel, in_specs=[whole(), whole()], out_specs=[who...  42 us
    ppermute x25, starting transfers between devices, shift(): lax.ppermute(value, axis, [(i, (i + step) % size) for i in range(size)])  36.3 us
    all_to_all x1, waiting for transfers between devices, body(): lax.all_to_all(terms.reshape(chips, piece, group_width), SAME_CORE, 0, 0,...  30.6 us
    all_to_all x1, starting transfers between devices, body(): lax.all_to_all(terms.reshape(chips, piece, group_width), SAME_CORE, 0, 0,...  12 us
    pallas_call x1, Pallas kernels, sketch_call(): pl.pallas_call(sketch_kernel, grid_spec=pltpu.PrefetchScalarGridSpec(num_...  11 us
    pallas_call x1, Pallas kernels, coeff_call(): pl.pallas_call(coeff_kernel, grid_spec=pltpu.PrefetchScalarGridSpec(num_s...  9.86 us
    pallas_call x1, Pallas kernels, gram_call(): pl.pallas_call(gram_kernel, in_specs=[pl.BlockSpec(memory_space=pltpu.SME...  9.82 us
  transfers between devices with their start and end apart: 26, of which 13 were waited for; matrix products, arithmetic and copies ran while one was open for 2% of the time, Pallas kernels for 24%

profile of v1, /device:TPU:1, one launch (start us, length us, event | category | flops | bytes accessed | tf_op | source)
XLA Modules:
  0.0 216.1 jit_solution(15885781367707989490)
XLA Ops:
  0.0 11.0 %sketch.1 = (bf16[2,4,2,320,256]{4,3,2,1,0:T(8,128)(2,1)}, bf16[2,800,1280]{2,1,0:T(8,128)(2,1)}) custom-call(s32[1]{0:T(128)} %bitcast.1.core_ref, bf16[2,800,5120]{2,1,0:T(8,128)(2,1)} %deltas_ref.3, bf16[800,128]{1,0:T(8,128)(2,1)} %sketch_ref.1), custom_call_target="tpu_custom_call" | custom-call | tf_op jit(solution)/shard_map/sketch/pallas_call | solution.py:50
  11.0 12.0 %all-to-all-start = ((bf16[64,80,256]{2,1,0:T(8,128)(2,1)}), bf16[64,80,256]{2,1,0:T(8,128)(2,1)S(1)}, u32[]{:S(2)}, u32[]{:S(2)}) async-start(bf16[64,80,256]{2,1,0:T(8,128)(2,1)} %bitcast.32), calls=%async_computation | async-start | bytes 5242880 | tf_op jit(solution)/shard_map/all_to_all | solution.py:277
  23.0 1.5 collective-permute-start
  24.5 30.6 %all-to-all-done = bf16[64,80,256]{2,1,0:T(8,128)(2,1)S(1)} async-done(((bf16[64,80,256]{2,1,0:T(8,128)(2,1)}), bf16[64,80,256]{2,1,0:T(8,128)(2,1)S(1)}, u32[]{:S(2)}, u32[]{:S(2)}) %all-to-all-start) | async-done | bytes 2621472 | tf_op jit(solution)/shard_map/all_to_all | solution.py:277
  55.0 0.3 bitcast_reduce_fusion
  55.4 0.6 collective-permute-start.1
  56.0 3.2 %collective-permute-start.2 = (bf16[80,512]{1,0:T(8,128)(2,1)S(1)}, bf16[80,512]{1,0:T(8,128)(2,1)S(1)}, u32[]{:S(2)}, u32[]{:S(2)}) collective-permute-start(bf16[80,512]{1,0:T(8,128)(2,1)S(1)} %pad_maximum_fusion.5), channel_id=1, source_target_pairs={{0,68},{4,0},{64,4},{68,64},{1,69},{5,1},{65,5},{69,65},{2,70},{6,... | collective-permute-start | bytes 245768 | tf_op jit(solution)/shard_map/ppermute | solution.py:27
  59.3 0.0 collective-permute-start.3
  59.3 1.0 collective-permute-done.1
  60.3 0.4 collective-permute-done.2
  60.7 3.0 %collective-permute-done.3 = bf16[80,512]{1,0:T(8,128)(2,1)S(1)} collective-permute-done((bf16[80,512]{1,0:T(8,128)(2,1)S(1)}, bf16[80,512]{1,0:T(8,128)(2,1)S(1)}, u32[]{:S(2)}, u32[]{:S(2)}) %collective-permute-start.3) | collective-permute-done | bytes 81952 | tf_op jit(solution)/shard_map/ppermute | solution.py:27
  63.8 5.3 %collective-permute-start.4 = (bf16[2,80,512]{2,1,0:T(8,128)(2,1)S(1)}, bf16[2,80,512]{2,1,0:T(8,128)(2,1)S(1)}, u32[]{:S(2)}, u32[]{:S(2)}) collective-permute-start(bf16[2,80,512]{2,1,0:T(8,128)(2,1)S(1)} %broadcast_select_fusion.2), channel_id=1, source_target_pairs={{0,32},{32,0},{1,33},{33,1},{2,34},{34,2},{3,35},{35,3},{4,36},{36... | collective-permute-start | bytes 491528 | tf_op jit(solution)/shard_map/ppermute | solution.py:27
  69.1 1.0 collective-permute-done.4
  70.2 0.1 collective-permute-start.6
  70.3 2.2 %collective-permute-start.5 = (bf16[2,80,512]{2,1,0:T(8,128)(2,1)S(1)}, bf16[2,80,512]{2,1,0:T(8,128)(2,1)S(1)}, u32[]{:S(2)}, u32[]{:S(2)}) collective-permute-start(bf16[2,80,512]{2,1,0:T(8,128)(2,1)S(1)} %get-tuple-element.20), channel_id=1, source_target_pairs={{0,8},{8,16},{16,24},{24,0},{1,9},{9,17},{17,25},{25,1},{2,10},{10... | collective-permute-start | bytes 491528 | tf_op jit(solution)/shard_map/ppermute | solution.py:27
  72.4 1.7 collective-permute-start.14
  74.1 0.0 collective-permute-start.13
  74.1 2.5 %collective-permute-done.6 = bf16[2,80,512]{2,1,0:T(8,128)(2,1)S(1)} collective-permute-done((bf16[2,80,512]{2,1,0:T(8,128)(2,1)S(1)}, bf16[2,80,512]{2,1,0:T(8,128)(2,1)S(1)}, u32[]{:S(2)}, u32[]{:S(2)}) %collective-permute-start.6) | collective-permute-done | bytes 163872 | tf_op jit(solution)/shard_map/ppermute | solution.py:27
  76.6 0.3 collective-permute-start.8
  76.9 0.0 collective-permute-done.5
  76.9 1.3 collective-permute-start.7
  78.2 2.2 %collective-permute-start.16 = (bf16[1,80,512]{2,1,0:T(8,128)(2,1)S(1)}, bf16[1,80,512]{2,1,0:T(8,128)(2,1)S(1)}, u32[]{:S(2)}, u32[]{:S(2)}) collective-permute-start(bf16[1,80,512]{2,1,0:T(8,128)(2,1)S(1)} %slice.47), channel_id=1, source_target_pairs={{0,3},{1,0},{2,1},{3,2},{4,7},{5,4},{6,5},{7,6},{8,11},{9,8},{10,9... | collective-permute-start | bytes 245768 | tf_op jit(solution)/shard_map/ppermute | solution.py:27
  80.4 0.1 collective-permute-start.15
  80.5 0.0 collective-permute-done.8
  80.5 1.0 collective-permute-done.7
  81.6 0.1 pad_maximum_fusion.1.a0
  81.6 0.0 copy-start.1
  81.7 0.6 collective-permute-start.9
  82.3 2.4 %collective-permute-start.10 = (bf16[4,2,80,512]{3,2,1,0:T(8,128)(2,1)S(1)}, bf16[4,2,80,512]{3,2,1,0:T(8,128)(2,1)S(1)}, u32[]{:S(2)}, u32[]{:S(2)}) collective-permute-start(bf16[4,2,80,512]{3,2,1,0:T(8,128)(2,1)S(1)} %pad_maximum_fusion.1.a0), channel_id=1, source_target_pairs={{0,3},{1,0},{2,1},{3,2},{4,7},{5,4},{6,5},{7,6},{8,11},{9,8},{10,9... | collective-permute-start | bytes 1966088 | tf_op jit(solution)/shard_map/ppermute | solution.py:27
  84.7 0.3 collective-permute-done.15
  85.0 0.1 pad_maximum_fusion.2.b0
  85.1 1.1 collective-permute-start.17
  86.3 1.6 collective-permute-start.18
  87.9 10.8 %collective-permute-done.9.a1 = bf16[4,2,80,512]{3,2,1,0:T(8,128)(2,1)S(1)} collective-permute-done((bf16[4,2,80,512]{3,2,1,0:T(8,128)(2,1)S(1)}, bf16[4,2,80,512]{3,2,1,0:T(8,128)(2,1)S(1)}, u32[]{:S(2)}, u32[]{:S(2)}) %collective-permute-start.9) | collective-permute-done | bytes 655392 | tf_op jit(solution)/shard_map/ppermute | solution.py:27
  98.7 0.8 slice.44
  99.5 0.0 collective-permute-start.11
  99.5 0.8 slice.45
  100.3 2.7 %collective-permute-start.12 = (bf16[2,2,80,512]{3,2,1,0:T(8,128)(2,1)}, bf16[2,2,80,512]{3,2,1,0:T(8,128)(2,1)}, u32[]{:S(2)}, u32[]{:S(2)}) collective-permute-start(bf16[2,2,80,512]{3,2,1,0:T(8,128)(2,1)} %slice.45), channel_id=1, source_target_pairs={{0,3},{1,0},{2,1},{3,2},{4,7},{5,4},{6,5},{7,6},{8,11},{9,8},{10,9... | collective-permute-start | bytes 983048 | tf_op jit(solution)/shard_map/ppermute | solution.py:27
  103.0 0.8 slice.48
  103.9 0.0 collective-permute-start.19
  103.9 0.8 copy-done.6
  104.7 2.9 %collective-permute-start.20 = (bf16[2,2,80,512]{3,2,1,0:T(8,128)(2,1)S(1)}, bf16[2,2,80,512]{3,2,1,0:T(8,128)(2,1)S(1)}, u32[]{:S(2)}, u32[]{:S(2)}) collective-permute-start(bf16[2,2,80,512]{3,2,1,0:T(8,128)(2,1)S(1)} %slice.49), channel_id=1, source_target_pairs={{0,24},{8,0},{16,8},{24,16},{1,25},{9,1},{17,9},{25,17},{2,26},{10... | collective-permute-start | bytes 983048 | tf_op jit(solution)/shard_map/ppermute | solution.py:27
  107.6 0.6 pad_add_fusion.at_ref
  108.3 3.0 %collective-permute-done.19.b3 = bf16[2,2,80,512]{3,2,1,0:T(8,128)(2,1)} collective-permute-done((bf16[2,2,80,512]{3,2,1,0:T(8,128)(2,1)}, bf16[2,2,80,512]{3,2,1,0:T(8,128)(2,1)}, u32[]{:S(2)}, u32[]{:S(2)}) %collective-permute-start.19) | collective-permute-done | bytes 327712 | tf_op jit(solution)/shard_map/ppermute | solution.py:27
  111.3 0.4 collective-permute-done.20.b4
  111.7 0.7 copy-done.7
  112.4 9.8 %gram.1 = (bf16[2,4,4,80,1024]{4,3,2,1,0:T(8,128)(2,1)}, bf16[1024,1024]{1,0:T(8,128)(2,1)}) custom-call(s32[2]{0:T(128)} %pad_add_fusion.at_ref, bf16[4,2,80,512]{3,2,1,0:T(8,128)(2,1)} %copy-done.1, bf16[4,2,80,512]{3,2,1,0:T(8,128)(2,1)} %copy-done.3, bf16[4,2,80,512]{3,2,1,0:T(8,128)(2,1)} %copy-done.4, ...), custom_call_target="tpu_custom_call" | custom-call | tf_op jit(solution)/shard_map/gram/pallas_call | solution.py:109
  122.2 0.0 collective-permute-done.pool_ref
  122.2 9.9 %coeff.1 = bf16[800,1024]{1,0:T(8,128)(2,1)} custom-call(s32[1]{0:T(128)} %bitcast.1.core_ref, bf16[2,800,5120]{2,1,0:T(8,128)(2,1)} %deltas_ref.3, bf16[2,800,1280]{2,1,0:T(8,128)(2,1)} %collective-permute-done.pool_ref, bf16[2,1280,1024]{2,1,0:T(8,128)(2,1)} %bitcast.30), custom_call_target="tpu_custom_call" | custom-call | tf_op jit(solution)/shard_map/coeff/pallas_call | solution.py:142
  132.1 1.3 constant_dynamic-slice_fusion
  133.4 4.3 %collective-permute-start.21 = (bf16[400,1024]{1,0:T(8,128)(2,1)S(1)}, bf16[400,1024]{1,0:T(8,128)(2,1)S(1)}, u32[]{:S(2)}, u32[]{:S(2)}) collective-permute-start(bf16[400,1024]{1,0:T(8,128)(2,1)S(1)} %constant_dynamic-slice_fusion), channel_id=1, source_target_pairs={{0,32},{32,0},{1,33},{33,1},{2,34},{34,2},{3,35},{35,3},{4,36},{36... | collective-permute-start | bytes 2457608 | tf_op jit(solution)/shard_map/ppermute | solution.py:27
  137.7 0.1 collective-permute-start.24
  137.8 2.1 collective-permute-done.21
  139.9 0.3 add_convert_fusion
  140.2 0.9 collective-permute-start.22
  141.1 20.1 %collective-permute-done.22 = bf16[400,1024]{1,0:T(8,128)(2,1)S(1)} collective-permute-done((bf16[400,1024]{1,0:T(8,128)(2,1)S(1)}, bf16[400,1024]{1,0:T(8,128)(2,1)S(1)}, u32[]{:S(2)}, u32[]{:S(2)}) %collective-permute-start.22) | collective-permute-done | bytes 819232 | tf_op jit(solution)/shard_map/ppermute | solution.py:27
  161.3 0.3 multiply_convert_fusion
  161.6 1.3 collective-permute-start.23
  162.8 0.0 collective-permute-done.24.other_ref
  162.9 42.0 %schulz.1 = (bf16[1024,1024]{1,0:T(8,128)(2,1)}, f32[8,128]{1,0:T(8,128)}) custom-call(bf16[1024,1024]{1,0:T(8,128)(2,1)} %get-tuple-element.14.own_ref, bf16[1024,1024]{1,0:T(8,128)(2,1)} %collective-permute-done.24.other_ref), custom_call_target="tpu_custom_call" | custom-call | flops 25769803776 | bytes 6291456 | tf_op jit(solution)/shard_map/schulz/pallas_call | solution.py:210
  204.8 0.0 collective-permute-done.23
  204.8 0.1 broadcast_select_fusion.1
  204.9 1.4 pad_maximum_fusion.refs_0_
  206.3 9.7 %merge.1 = bf16[800,1280]{1,0:T(8,128)(2,1)} custom-call(s32[1]{0:T(128)} %bitcast.at, bf16[800,1024]{1,0:T(8,128)(2,1)} %pad_maximum_fusion.refs_0_, bf16[1024,1024]{1,0:T(8,128)(2,1)} %get-tuple-element.15.refs_1_, f32[8,128]{1,0:T(8,128)} %get-tuple-element.16.refs_2_, bf16[2,1280,1024]{2,1,0:T(8,128)(2,1)} %bitcast.31), custom_call_target="tpu_custom_call" | custom-call | tf_op jit(solution)/shard_map/merge/pallas_call | solution.py:235
  (34 shorter events, 0.3 us)
Async XLA Ops:
  11.0 44.0 %all-to-all-start = ((bf16[64,80,256]{2,1,0:T(8,128)(2,1)}), bf16[64,80,256]{2,1,0:T(8,128)(2,1)S(1)}, u32[]{:S(2)}, u32[]{:S(2)}) async-start(bf16[64,80,256]{2,1,0:T(8,128)(2,1)} %bitcast.32), calls=%async_computation | async-start | bytes 5242880 | tf_op jit(solution)/shard_map/all_to_all | solution.py:277
  23.0 99.3 %collective-permute-start = (bf16[2,800,1280]{2,1,0:T(8,128)(2,1)}, bf16[2,800,1280]{2,1,0:T(8,128)(2,1)}, u32[]{:S(2)}, u32[]{:S(2)}) collective-permute-start(bf16[2,800,1280]{2,1,0:T(8,128)(2,1)} %get-tuple-element.11), channel_id=1, source_target_pairs={{0,32},{32,0},{1,33},{33,1},{2,34},{34,2},{3,35},{35,3},{4,36},{36... | collective-permute-start | bytes 12288008 | tf_op jit(solution)/shard_map/ppermute | solution.py:27
  55.4 4.9 %collective-permute-start.1 = (bf16[80,512]{1,0:T(8,128)(2,1)S(1)}, bf16[80,512]{1,0:T(8,128)(2,1)S(1)}, u32[]{:S(2)}, u32[]{:S(2)}) collective-permute-start(bf16[80,512]{1,0:T(8,128)(2,1)S(1)} %pad_maximum_fusion.5), channel_id=1, source_target_pairs={{0,64},{4,68},{64,0},{68,4},{1,65},{5,69},{65,1},{69,5},{2,66},{6,... | collective-permute-start | bytes 245768 | tf_op jit(solution)/shard_map/ppermute | solution.py:27
  56.0 4.7 %collective-permute-start.2 = (bf16[80,512]{1,0:T(8,128)(2,1)S(1)}, bf16[80,512]{1,0:T(8,128)(2,1)S(1)}, u32[]{:S(2)}, u32[]{:S(2)}) collective-permute-start(bf16[80,512]{1,0:T(8,128)(2,1)S(1)} %pad_maximum_fusion.5), channel_id=1, source_target_pairs={{0,68},{4,0},{64,4},{68,64},{1,69},{5,1},{65,5},{69,65},{2,70},{6,... | collective-permute-start | bytes 245768 | tf_op jit(solution)/shard_map/ppermute | solution.py:27
  59.3 4.5 %collective-permute-start.3 = (bf16[80,512]{1,0:T(8,128)(2,1)S(1)}, bf16[80,512]{1,0:T(8,128)(2,1)S(1)}, u32[]{:S(2)}, u32[]{:S(2)}) collective-permute-start(bf16[80,512]{1,0:T(8,128)(2,1)S(1)} %pad_maximum_fusion.5), channel_id=1, source_target_pairs={{0,4},{4,64},{64,68},{68,0},{1,5},{5,65},{65,69},{69,1},{2,6},{6,6... | collective-permute-start | bytes 245768 | tf_op jit(solution)/shard_map/ppermute | solution.py:27
  63.8 6.3 %collective-permute-start.4 = (bf16[2,80,512]{2,1,0:T(8,128)(2,1)S(1)}, bf16[2,80,512]{2,1,0:T(8,128)(2,1)S(1)}, u32[]{:S(2)}, u32[]{:S(2)}) collective-permute-start(bf16[2,80,512]{2,1,0:T(8,128)(2,1)S(1)} %broadcast_select_fusion.2), channel_id=1, source_target_pairs={{0,32},{32,0},{1,33},{33,1},{2,34},{34,2},{3,35},{35,3},{4,36},{36... | collective-permute-start | bytes 491528 | tf_op jit(solution)/shard_map/ppermute | solution.py:27
  70.2 6.4 %collective-permute-start.6 = (bf16[2,80,512]{2,1,0:T(8,128)(2,1)S(1)}, bf16[2,80,512]{2,1,0:T(8,128)(2,1)S(1)}, u32[]{:S(2)}, u32[]{:S(2)}) collective-permute-start(bf16[2,80,512]{2,1,0:T(8,128)(2,1)S(1)} %get-tuple-element.20), channel_id=1, source_target_pairs={{0,24},{8,0},{16,8},{24,16},{1,25},{9,1},{17,9},{25,17},{2,26},{10... | collective-permute-start | bytes 491528 | tf_op jit(solution)/shard_map/ppermute | solution.py:27
  70.3 6.6 %collective-permute-start.5 = (bf16[2,80,512]{2,1,0:T(8,128)(2,1)S(1)}, bf16[2,80,512]{2,1,0:T(8,128)(2,1)S(1)}, u32[]{:S(2)}, u32[]{:S(2)}) collective-permute-start(bf16[2,80,512]{2,1,0:T(8,128)(2,1)S(1)} %get-tuple-element.20), channel_id=1, source_target_pairs={{0,8},{8,16},{16,24},{24,0},{1,9},{9,17},{17,25},{25,1},{2,10},{10... | collective-permute-start | bytes 491528 | tf_op jit(solution)/shard_map/ppermute | solution.py:27
  72.4 5.8 %collective-permute-start.14 = (bf16[2,80,512]{2,1,0:T(8,128)(2,1)S(1)}, bf16[2,80,512]{2,1,0:T(8,128)(2,1)S(1)}, u32[]{:S(2)}, u32[]{:S(2)}) collective-permute-start(bf16[2,80,512]{2,1,0:T(8,128)(2,1)S(1)} %get-tuple-element.19), channel_id=1, source_target_pairs={{0,3},{1,0},{2,1},{3,2},{4,7},{5,4},{6,5},{7,6},{8,11},{9,8},{10,9... | collective-permute-start | bytes 491528 | tf_op jit(solution)/shard_map/ppermute | solution.py:27
  74.1 6.3 %collective-permute-start.13 = (bf16[2,80,512]{2,1,0:T(8,128)(2,1)S(1)}, bf16[2,80,512]{2,1,0:T(8,128)(2,1)S(1)}, u32[]{:S(2)}, u32[]{:S(2)}) collective-permute-start(bf16[2,80,512]{2,1,0:T(8,128)(2,1)S(1)} %get-tuple-element.19), channel_id=1, source_target_pairs={{0,1},{1,2},{2,3},{3,0},{4,5},{5,6},{6,7},{7,4},{8,9},{9,10},{10,1... | collective-permute-start | bytes 491528 | tf_op jit(solution)/shard_map/ppermute | solution.py:27
  76.6 3.9 %collective-permute-start.8 = (bf16[1,80,512]{2,1,0:T(8,128)(2,1)S(1)}, bf16[1,80,512]{2,1,0:T(8,128)(2,1)S(1)}, u32[]{:S(2)}, u32[]{:S(2)}) collective-permute-start(bf16[1,80,512]{2,1,0:T(8,128)(2,1)S(1)} %slice.43), channel_id=1, source_target_pairs={{0,24},{8,0},{16,8},{24,16},{1,25},{9,1},{17,9},{25,17},{2,26},{10... | collective-permute-start | bytes 245768 | tf_op jit(solution)/shard_map/ppermute | solution.py:27
  76.9 4.6 %collective-permute-start.7 = (bf16[1,80,512]{2,1,0:T(8,128)(2,1)S(1)}, bf16[1,80,512]{2,1,0:T(8,128)(2,1)S(1)}, u32[]{:S(2)}, u32[]{:S(2)}) collective-permute-start(bf16[1,80,512]{2,1,0:T(8,128)(2,1)S(1)} %slice.42), channel_id=1, source_target_pairs={{0,8},{8,16},{16,24},{24,0},{1,9},{9,17},{17,25},{25,1},{2,10},{10... | collective-permute-start | bytes 245768 | tf_op jit(solution)/shard_map/ppermute | solution.py:27
  78.2 6.5 %collective-permute-start.16 = (bf16[1,80,512]{2,1,0:T(8,128)(2,1)S(1)}, bf16[1,80,512]{2,1,0:T(8,128)(2,1)S(1)}, u32[]{:S(2)}, u32[]{:S(2)}) collective-permute-start(bf16[1,80,512]{2,1,0:T(8,128)(2,1)S(1)} %slice.47), channel_id=1, source_target_pairs={{0,3},{1,0},{2,1},{3,2},{4,7},{5,4},{6,5},{7,6},{8,11},{9,8},{10,9... | collective-permute-start | bytes 245768 | tf_op jit(solution)/shard_map/ppermute | solution.py:27
  80.4 4.6 %collective-permute-start.15 = (bf16[1,80,512]{2,1,0:T(8,128)(2,1)S(1)}, bf16[1,80,512]{2,1,0:T(8,128)(2,1)S(1)}, u32[]{:S(2)}, u32[]{:S(2)}) collective-permute-start(bf16[1,80,512]{2,1,0:T(8,128)(2,1)S(1)} %slice.46), channel_id=1, source_target_pairs={{0,1},{1,2},{2,3},{3,0},{4,5},{5,6},{6,7},{7,4},{8,9},{9,10},{10,1... | collective-permute-start | bytes 245768 | tf_op jit(solution)/shard_map/ppermute | solution.py:27
  81.6 22.2 %copy-start.1 = (bf16[4,2,80,512]{3,2,1,0:T(8,128)(2,1)}, bf16[4,2,80,512]{3,2,1,0:T(8,128)(2,1)S(1)}, u32[]{:S(2)}) copy-start(bf16[4,2,80,512]{3,2,1,0:T(8,128)(2,1)S(1)} %pad_maximum_fusion.1.a0) | copy-start | bytes 1966084
  81.7 17.1 %collective-permute-start.9 = (bf16[4,2,80,512]{3,2,1,0:T(8,128)(2,1)S(1)}, bf16[4,2,80,512]{3,2,1,0:T(8,128)(2,1)S(1)}, u32[]{:S(2)}, u32[]{:S(2)}) collective-permute-start(bf16[4,2,80,512]{3,2,1,0:T(8,128)(2,1)S(1)} %pad_maximum_fusion.1.a0), channel_id=1, source_target_pairs={{0,1},{1,2},{2,3},{3,0},{4,5},{5,6},{6,7},{7,4},{8,9},{9,10},{10,1... | collective-permute-start | bytes 1966088 | tf_op jit(solution)/shard_map/ppermute | solution.py:27
  82.3 17.3 %collective-permute-start.10 = (bf16[4,2,80,512]{3,2,1,0:T(8,128)(2,1)S(1)}, bf16[4,2,80,512]{3,2,1,0:T(8,128)(2,1)S(1)}, u32[]{:S(2)}, u32[]{:S(2)}) collective-permute-start(bf16[4,2,80,512]{3,2,1,0:T(8,128)(2,1)S(1)} %pad_maximum_fusion.1.a0), channel_id=1, source_target_pairs={{0,3},{1,0},{2,1},{3,2},{4,7},{5,4},{6,5},{7,6},{8,11},{9,8},{10,9... | collective-permute-start | bytes 1966088 | tf_op jit(solution)/shard_map/ppermute | solution.py:27
  85.1 26.6 %copy-start.2 = (bf16[4,2,80,512]{3,2,1,0:T(8,128)(2,1)}, bf16[4,2,80,512]{3,2,1,0:T(8,128)(2,1)S(1)}, u32[]{:S(2)}) copy-start(bf16[4,2,80,512]{3,2,1,0:T(8,128)(2,1)S(1)} %pad_maximum_fusion.2.b0) | copy-start | bytes 1966084
  85.1 17.9 %collective-permute-start.17 = (bf16[4,2,80,512]{3,2,1,0:T(8,128)(2,1)S(1)}, bf16[4,2,80,512]{3,2,1,0:T(8,128)(2,1)S(1)}, u32[]{:S(2)}, u32[]{:S(2)}) collective-permute-start(bf16[4,2,80,512]{3,2,1,0:T(8,128)(2,1)S(1)} %pad_maximum_fusion.2.b0), channel_id=1, source_target_pairs={{0,8},{8,16},{16,24},{24,0},{1,9},{9,17},{17,25},{25,1},{2,10},{10... | collective-permute-start | bytes 1966088 | tf_op jit(solution)/shard_map/ppermute | solution.py:27
  86.3 17.6 %collective-permute-start.18 = (bf16[4,2,80,512]{3,2,1,0:T(8,128)(2,1)S(1)}, bf16[4,2,80,512]{3,2,1,0:T(8,128)(2,1)S(1)}, u32[]{:S(2)}, u32[]{:S(2)}) collective-permute-start(bf16[4,2,80,512]{3,2,1,0:T(8,128)(2,1)S(1)} %pad_maximum_fusion.2.b0), channel_id=1, source_target_pairs={{0,24},{8,0},{16,8},{24,16},{1,25},{9,1},{17,9},{25,17},{2,26},{10... | collective-permute-start | bytes 1966088 | tf_op jit(solution)/shard_map/ppermute | solution.py:27
  98.7 12.9 %copy-start.3 = (bf16[4,2,80,512]{3,2,1,0:T(8,128)(2,1)}, bf16[4,2,80,512]{3,2,1,0:T(8,128)(2,1)S(1)}, u32[]{:S(2)}) copy-start(bf16[4,2,80,512]{3,2,1,0:T(8,128)(2,1)S(1)} %collective-permute-done.9.a1) | copy-start | bytes 1966084
  99.5 8.8 %collective-permute-start.11 = (bf16[2,2,80,512]{3,2,1,0:T(8,128)(2,1)}, bf16[2,2,80,512]{3,2,1,0:T(8,128)(2,1)}, u32[]{:S(2)}, u32[]{:S(2)}) collective-permute-start(bf16[2,2,80,512]{3,2,1,0:T(8,128)(2,1)} %slice.44), channel_id=1, source_target_pairs={{0,1},{1,2},{2,3},{3,0},{4,5},{5,6},{6,7},{7,4},{8,9},{9,10},{10,1... | collective-permute-start | bytes 983048 | tf_op jit(solution)/shard_map/ppermute | solution.py:27
  99.5 12.1 %copy-start.4 = (bf16[4,2,80,512]{3,2,1,0:T(8,128)(2,1)}, bf16[4,2,80,512]{3,2,1,0:T(8,128)(2,1)S(1)}, u32[]{:S(2)}) copy-start(bf16[4,2,80,512]{3,2,1,0:T(8,128)(2,1)S(1)} %collective-permute-done.10.a2) | copy-start | bytes 1966084
  100.3 8.0 %collective-permute-start.12 = (bf16[2,2,80,512]{3,2,1,0:T(8,128)(2,1)}, bf16[2,2,80,512]{3,2,1,0:T(8,128)(2,1)}, u32[]{:S(2)}, u32[]{:S(2)}) collective-permute-start(bf16[2,2,80,512]{3,2,1,0:T(8,128)(2,1)} %slice.45), channel_id=1, source_target_pairs={{0,3},{1,0},{2,1},{3,2},{4,7},{5,4},{6,5},{7,6},{8,11},{9,8},{10,9... | collective-permute-start | bytes 983048 | tf_op jit(solution)/shard_map/ppermute | solution.py:27
  103.0 8.7 %copy-start.5 = (bf16[4,2,80,512]{3,2,1,0:T(8,128)(2,1)}, bf16[4,2,80,512]{3,2,1,0:T(8,128)(2,1)S(1)}, u32[]{:S(2)}) copy-start(bf16[4,2,80,512]{3,2,1,0:T(8,128)(2,1)S(1)} %collective-permute-done.17.b1) | copy-start | bytes 1966084
  103.9 7.5 %collective-permute-start.19 = (bf16[2,2,80,512]{3,2,1,0:T(8,128)(2,1)}, bf16[2,2,80,512]{3,2,1,0:T(8,128)(2,1)}, u32[]{:S(2)}, u32[]{:S(2)}) collective-permute-start(bf16[2,2,80,512]{3,2,1,0:T(8,128)(2,1)} %slice.48), channel_id=1, source_target_pairs={{0,8},{8,16},{16,24},{24,0},{1,9},{9,17},{17,25},{25,1},{2,10},{10... | collective-permute-start | bytes 983048 | tf_op jit(solution)/shard_map/ppermute | solution.py:27
  103.9 0.8 copy-start.6
  104.7 6.9 %collective-permute-start.20 = (bf16[2,2,80,512]{3,2,1,0:T(8,128)(2,1)S(1)}, bf16[2,2,80,512]{3,2,1,0:T(8,128)(2,1)S(1)}, u32[]{:S(2)}, u32[]{:S(2)}) collective-permute-start(bf16[2,2,80,512]{3,2,1,0:T(8,128)(2,1)S(1)} %slice.49), channel_id=1, source_target_pairs={{0,24},{8,0},{16,8},{24,16},{1,25},{9,1},{17,9},{25,17},{2,26},{10... | collective-permute-start | bytes 983048 | tf_op jit(solution)/shard_map/ppermute | solution.py:27
  111.7 0.7 copy-start.7
  132.1 7.8 %copy-start = (bf16[800,1024]{1,0:T(8,128)(2,1)S(1)}, bf16[800,1024]{1,0:T(8,128)(2,1)}, u32[]{:S(2)}) copy-start(bf16[800,1024]{1,0:T(8,128)(2,1)} %coeff.1) | copy-start | bytes 4915204
  133.4 6.5 %collective-permute-start.21 = (bf16[400,1024]{1,0:T(8,128)(2,1)S(1)}, bf16[400,1024]{1,0:T(8,128)(2,1)S(1)}, u32[]{:S(2)}, u32[]{:S(2)}) collective-permute-start(bf16[400,1024]{1,0:T(8,128)(2,1)S(1)} %constant_dynamic-slice_fusion), channel_id=1, source_target_pairs={{0,32},{32,0},{1,33},{33,1},{2,34},{34,2},{3,35},{35,3},{4,36},{36... | collective-permute-start | bytes 2457608 | tf_op jit(solution)/shard_map/ppermute | solution.py:27
  137.7 25.1 %collective-permute-start.24 = (bf16[1024,1024]{1,0:T(8,128)(2,1)}, bf16[1024,1024]{1,0:T(8,128)(2,1)}, u32[]{:S(2)}, u32[]{:S(2)}) collective-permute-start(bf16[1024,1024]{1,0:T(8,128)(2,1)} %get-tuple-element.14.own_ref), channel_id=1, source_target_pairs={{0,32},{32,0},{1,33},{33,1},{2,34},{34,2},{3,35},{35,3},{4,36},{36... | collective-permute-start | bytes 6291464 | tf_op jit(solution)/shard_map/ppermute | solution.py:27
  140.2 21.0 %collective-permute-start.22 = (bf16[400,1024]{1,0:T(8,128)(2,1)S(1)}, bf16[400,1024]{1,0:T(8,128)(2,1)S(1)}, u32[]{:S(2)}, u32[]{:S(2)}) collective-permute-start(bf16[400,1024]{1,0:T(8,128)(2,1)S(1)} %add_convert_fusion), channel_id=1, source_target_pairs={{0,64},{64,0},{1,65},{65,1},{2,66},{66,2},{3,67},{67,3},{4,68},{68... | collective-permute-start | bytes 2457608 | tf_op jit(solution)/shard_map/ppermute | solution.py:27
  161.6 43.3 %collective-permute-start.23 = (bf16[400,1024]{1,0:T(8,128)(2,1)S(1)}, bf16[400,1024]{1,0:T(8,128)(2,1)S(1)}, u32[]{:S(2)}, u32[]{:S(2)}) collective-permute-start(bf16[400,1024]{1,0:T(8,128)(2,1)S(1)} %multiply_convert_fusion), channel_id=1, source_target_pairs={{0,32},{32,0},{1,33},{33,1},{2,34},{34,2},{3,35},{35,3},{4,36},{36... | collective-permute-start | bytes 2457608 | tf_op jit(solution)/shard_map/ppermute | solution.py:27
